TPU v7x, 32 devices: a whole 2x2x4 slice. The times are simulated.
32 devices in a mesh: grp: 2 (over y), dom: 4 (over z), lvl: 2 (over x), sub: 2 (over core).
Axes of the slice: x: 2, y: 2, z: 4, core: 2. Of those that a mesh axis runs over, the one named last changes fastest.
Arguments:
- node_latents: bfloat16 [24576, 512], P(('grp', 'dom', 'lvl', 'sub')), parts along dimension 0, may hold values from -6 to 6
- coarse_latents: bfloat16 [2048, 512], P(('grp', 'dom', 'lvl', 'sub')), parts along dimension 0, may hold values from -6 to 6
- cotangent: bfloat16 [24576, 512], P(('grp', 'dom', 'lvl', 'sub')), parts along dimension 0, may hold values from -6 to 6
- w_message: bfloat16 [512, 512], replicated, may hold values from -0.25 to 0.25
- w_coarse: bfloat16 [512, 512], replicated, may hold values from -0.25 to 0.25
- w_update: bfloat16 [512, 512], replicated, may hold values from -0.25 to 0.25
- mask_words: int32 [24576, 8], P(('grp', 'dom', 'lvl', 'sub')), parts along dimension 0, may hold values from 0 to 65535
- tile_index: int32 [96, 16], P(('grp', 'dom', 'lvl', 'sub')), parts along dimension 0, may hold values from 0 to 767
- partner: int32 [6, 4], P('grp'), parts along dimension 0, may hold values from 0 to 3, as said below
- assignment: int32 [24576], P(('grp', 'dom', 'lvl', 'sub')), parts along dimension 0, may hold values from 0 to 127
- live_counts: int32 [32], P(('grp', 'dom', 'lvl', 'sub')), parts along dimension 0, may hold values from 192 to 768
Outputs:
- updated: bfloat16 [24576, 512], P(('grp', 'dom', 'lvl', 'sub')), parts along dimension 0
- d_nodes: bfloat16 [24576, 512], P(('grp', 'dom', 'lvl', 'sub')), parts along dimension 0
- d_coarse: bfloat16 [2048, 512], P(('grp', 'dom', 'lvl', 'sub')), parts along dimension 0
There are 2 independent parts, one for each index of `grp`. A program takes and returns all parts, laid end to end along the dimension named above; an argument that names none is the same for every part. Nothing has to cross between parts.
Inputs may be any that keep to these rules, and one draw needn't show every extreme that they name: In each of the 3 rounds partner of partner is the part itself; a part may be its own partner in at most one round, and then its tile rows receive its own tile; a part's partners in different rounds all differ.
All inputs are finite; a program needn't handle non-finite values.
Results may differ from a plain program's by a relative error of at most 0.0071.
Values may be sent and summed in bfloat16 or wider, within the bound.
A program may use at most 64 MiB of HBM per device.

v0:
```python
import jax
import jax.numpy as jnp
import numpy as np
from jax import lax
from jax.sharding import PartitionSpec as P


def silu_slope(values):
    logistic = jax.nn.sigmoid(values)
    return logistic * (1.0 + values * (1.0 - logistic))


def unpack_mask(words):
    columns = np.arange(128)
    picked = jnp.take(words, jnp.asarray(columns // 16, dtype=jnp.int32), axis=1)
    shifts = jnp.asarray(columns % 16, dtype=jnp.int32)
    return jnp.bitwise_and(jnp.right_shift(picked, shifts[None, :]), 1)


def trade_tiles(values, tile_index, partner):
    own_index = lax.axis_index("dom")
    column = lax.dynamic_index_in_dim(partner, own_index, 1, keepdims=False)
    rounds = tile_index.shape[0]
    tile_rows = values[tile_index]
    everyone = lax.all_gather(tile_rows, "dom", axis=0, tiled=True)
    arrived = everyone[column * rounds + jnp.arange(rounds, dtype=jnp.int32)]
    flat_index = tile_index.reshape(-1)
    landed = arrived.reshape(flat_index.shape[0], values.shape[1]).astype(jnp.float32)
    return jnp.zeros((values.shape[0], values.shape[1]), jnp.float32).at[flat_index].add(landed)


def on_device(
    node_latents,
    coarse_latents,
    cotangent,
    w_message,
    w_coarse,
    w_update,
    mask_words,
    tile_index,
    partner,
    assignment,
    live_counts,
):
    node_rows, hidden = node_latents.shape
    coarse_rows = coarse_latents.shape[0]
    block_count = node_rows // 128
    live = (jnp.arange(node_rows, dtype=jnp.int32) < live_counts[0])[:, None]
    pre_msg = jnp.dot(node_latents, w_message, preferred_element_type=jnp.float32)
    message = jnp.where(live, jax.nn.silu(pre_msg), 0.0).astype(jnp.bfloat16)
    pre_crs = jnp.dot(coarse_latents, w_coarse, preferred_element_type=jnp.float32)
    coarse_msg = jax.nn.silu(pre_crs).astype(jnp.bfloat16)
    adjacency = unpack_mask(mask_words).astype(jnp.bfloat16).reshape(block_count, 128, 128)

    def local_sum(values, form):
        blocks = values.reshape(block_count, 128, hidden)
        return jnp.einsum(form, adjacency, blocks, preferred_element_type=jnp.float32).reshape(
            node_rows, hidden
        )

    piece = lax.all_gather(coarse_msg, "lvl", axis=0, tiled=True)
    columns = jnp.arange(piece.shape[0], dtype=jnp.int32)
    picker = (assignment[:, None] == columns[None, :]).astype(jnp.bfloat16)
    coarse_term = jnp.dot(picker, piece, preferred_element_type=jnp.float32)
    aggregate = (
        0.125 * local_sum(message, "bij,bjh->bih")
        + trade_tiles(message, tile_index, partner)
        + coarse_term
    )
    aggregate = aggregate.astype(jnp.bfloat16)
    pre_upd = jnp.dot(aggregate, w_update, preferred_element_type=jnp.float32)
    updated = (
        node_latents.astype(jnp.float32) + jnp.where(live, jax.nn.silu(pre_upd), 0.0)
    ).astype(jnp.bfloat16)
    d_pre_upd = jnp.where(live, cotangent.astype(jnp.float32) * silu_slope(pre_upd), 0.0).astype(
        jnp.bfloat16
    )
    d_agg = jnp.dot(d_pre_upd, jnp.transpose(w_update), preferred_element_type=jnp.float32).astype(
        jnp.bfloat16
    )
    d_message = 0.125 * local_sum(d_agg, "bji,bjh->bih") + trade_tiles(d_agg, tile_index, partner)
    d_pre_msg = jnp.where(live, d_message * silu_slope(pre_msg), 0.0).astype(jnp.bfloat16)
    d_nodes = (
        cotangent.astype(jnp.float32)
        + jnp.dot(d_pre_msg, jnp.transpose(w_message), preferred_element_type=jnp.float32)
    ).astype(jnp.bfloat16)
    columns = jnp.arange(coarse_rows * lax.axis_size("lvl"), dtype=jnp.int32)
    picker = (assignment[:, None] == columns[None, :]).astype(jnp.bfloat16)
    d_coarse_msg = lax.psum_scatter(
        lax.dot_general(
            picker, d_agg, (((0,), (0,)), ((), ())), preferred_element_type=jnp.float32
        ),
        "lvl",
        scatter_dimension=0,
        tiled=True,
    )
    d_pre_crs = (d_coarse_msg * silu_slope(pre_crs)).astype(jnp.bfloat16)
    d_coarse = jnp.dot(
        d_pre_crs, jnp.transpose(w_coarse), preferred_element_type=jnp.float32
    ).astype(jnp.bfloat16)
    return (updated, d_nodes, d_coarse)


def solution(mesh):
    return jax.shard_map(
        on_device,
        mesh=mesh,
        in_specs=(
            P(("grp", "dom", "lvl", "sub"), None),
            P(("grp", "dom", "lvl", "sub"), None),
            P(("grp", "dom", "lvl", "sub"), None),
            P(),
            P(),
            P(),
            P(("grp", "dom", "lvl", "sub"), None),
            P(("grp", "dom", "lvl", "sub"), None),
            P("grp", None),
            P(("grp", "dom", "lvl", "sub")),
            P(("grp", "dom", "lvl", "sub")),
        ),
        out_specs=(
            P(("grp", "dom", "lvl", "sub"), None),
            P(("grp", "dom", "lvl", "sub"), None),
            P(("grp", "dom", "lvl", "sub"), None),
        ),
        check_vma=False,
    )
```

profile of v0, /device:TPU:0, one launch (start us, length us, event | category | flops | bytes accessed | tf_op | source)
XLA Modules:
  0.0 73.1 jit_solution(8366529256725927013)
XLA Ops:
  7.2 0.0 copy-start
  7.2 0.0 reduce-scatter.2.cloned.1.call-start
  7.2 0.8 %reshape.81 = s32[48,1]{0,1:T(1,128)S(1)} reshape(s32[3,16]{1,0:T(4,128)} %param.20) | data formatting | bytes 384 | tf_op jit(solution)/shard_map/reshape | solution.py:27
  8.1 0.7 compare_select_fusion.1
  9.4 0.1 reshape.95
  9.5 0.9 %fusion.15 = s32[3]{0:T(128)S(1)} fusion(s32[3,4]{1,0:T(4,128)} %param.21, s32[]{:T(128)S(6)} %select_n.53), kind=kLoop, calls=%fused_computation.45 | loop fusion | flops 15 | bytes 28 | tf_op jit(solution)/shard_map/select_n | solution.py:26
  10.4 0.7 pad_clamp_fusion.2
  11.0 2.0 %multiply_convert_fusion.1 = (bf16[64,512]{1,0:T(8,128)(2,1)S(1)}, f32[64,512]{1,0:T(8,128)}) fusion(bf16[64,512]{1,0:T(8,128)(2,1)} %param.14, bf16[512,512]{1,0:T(8,128)(2,1)} %param.17), kind=kOutput, calls=%fused_computation.31 | convolution fusion | flops 33718272 | bytes 786432 | tf_op jit(solution)/shard_map/dot_general | solution.py:51
  13.0 5.8 %all_gather.9 = bf16[128,512]{1,0:T(8,128)(2,1)S(1)} all-gather(bf16[64,512]{1,0:T(8,128)(2,1)S(1)} %get-tuple-element.5), channel_id=1, replica_groups=mesh['grp'=2,'dom'=4,'lvl'=2,'sub'=2] {'lvl'}, dimensions={0}, use_global_device_ids=true | all-gather | bytes 196608 | tf_op jit(solution)/shard_map/all_gather | solution.py:61
  18.8 0.8 %gather_fusion = s32[128,768]{1,0:T(8,128)S(1)} fusion(s32[768,8]{0,1:T(8,128)S(1)} %copy-done.1, s32[1024]{0:T(1024)S(1)} %pad_clamp_fusion.2), kind=kCustom, calls=%fused_computation | custom fusion | bytes 786944 | tf_op jit(solution)/shard_map/jit(_take)/gather | solution.py:15
  19.6 0.2 copy.20
  19.8 0.1 copy-done.4
  20.0 0.1 copy-done.8
  20.1 1.9 %select_convert_fusion.1 = (bf16[768,512]{1,0:T(8,128)(2,1)S(1)}, f32[768,512]{1,0:T(8,128)}) fusion(pred[768]{0:T(1024)(128)(4,1)S(1)} %iota_compare_fusion.3, bf16[768,512]{1,0:T(8,128)(2,1)S(1)} %copy-done.4, bf16[512,512]{1,0:T(8,128)(2,1)S(1)} %copy-done.8), kind=kOutput, calls=%fused_computation.16 | convolution fusion | flops 405012480 | bytes 3670784 | tf_op jit(solution)/shard_map/dot_general | solution.py:49
  22.0 0.7 gather_fusion.1
  22.6 14.5 %all-gather = bf16[12,16,512]{2,1,0:T(8,128)(2,1)S(1)} all-gather(bf16[3,16,512]{2,1,0:T(8,128)(2,1)S(1)} %bitcast.38), channel_id=2, replica_groups=mesh['grp'=2,'dom'=4,'lvl'=2,'sub'=2] {'dom'}, dimensions={0}, use_global_device_ids=true | all-gather | bytes 245760 | tf_op jit(solution)/shard_map/all_gather | solution.py:25
  37.1 0.5 gather_fusion.2
  37.7 0.4 convolution_multiply_fusion.1
  38.1 0.4 bitcast_add_fusion
  38.5 1.5 %scatter_custom_fusion = f32[768,512]{1,0:T(8,128)S(1)} fusion(f32[768,512]{1,0:T(8,128)S(1)} %bitcast_add_fusion, s32[48]{0:T(128)S(1)} %fusion.16, bf16[48,512]{1,0:T(8,128)(2,1)S(1)} %bitcast.35), kind=kCustom, calls=%fused_computation.35 | custom fusion | flops 49152 | bytes 1622016 | tf_op jit(solution)/shard_map/scatter-add | solution.py:29
  40.0 0.0 copy-start.6
  40.0 1.7 %add_convert_fusion = (bf16[768,512]{1,0:T(8,128)(2,1)}, f32[768,512]{1,0:T(8,128)S(1)}) fusion(bf16[768,512]{1,0:T(8,128)(2,1)S(1)} %copy-done.5, pred[768]{0:T(1024)(128)(4,1)S(1)} %iota_compare_fusion.3, bf16[512,512]{1,0:T(8,128)(2,1)S(1)} %copy-done, f32[768,512]{1,0:T(8,128)S(1)} %scatter_custom_fusion), kind=kOutput, calls=%fused_computation.14 | convolution fusion | flops 406192128 | bytes 5243648 | tf_op jit(solution)/shard_map/dot_general | solution.py:71
  41.7 0.8 %convolution_convert_fusion = bf16[768,512]{1,0:T(8,128)(2,1)S(1)} fusion(bf16[512,512]{1,0:T(8,128)(2,1)S(1)} %copy-done, bf16[768,512]{1,0:T(8,128)(2,1)S(1)} %copy-done.6, f32[768,512]{1,0:T(8,128)S(1)} %get-tuple-element.8, pred[768]{0:T(1024)(128)(4,1)S(1)} %iota_compare_fusion.3), kind=kOutput, calls=%fused_computation.20 | convolution fusion | flops 407371776 | bytes 3670784 | tf_op jit(solution)/shard_map/dot_general | solution.py:78
  42.6 1.2 %fusion.7 = f32[128,512]{1,0:T(8,128)} fusion(bf16[768,512]{1,0:T(8,128)(2,1)S(1)} %convolution_convert_fusion, s32[768]{0:T(1024)S(1)} %copy-done.2), kind=kOutput, calls=%fused_computation.26 | convolution fusion | flops 100761600 | bytes 1051648 | tf_op jit(solution)/shard_map/dot_general | solution.py:90
  43.8 0.0 reduce-scatter.2.cloned.1.call-update
  43.8 0.7 gather_fusion.3
  44.5 0.4 convolution_multiply_fusion
  44.9 14.0 %all-gather.1 = bf16[12,16,512]{2,1,0:T(8,128)(2,1)S(1)} all-gather(bf16[3,16,512]{2,1,0:T(8,128)(2,1)S(1)} %bitcast.37), channel_id=3, replica_groups=mesh['grp'=2,'dom'=4,'lvl'=2,'sub'=2] {'dom'}, dimensions={0}, use_global_device_ids=true | all-gather | bytes 245760 | tf_op jit(solution)/shard_map/all_gather | solution.py:25
  58.9 0.5 gather_fusion.4
  59.4 1.5 %scatter_custom_fusion.1 = f32[768,512]{1,0:T(8,128)S(1)} fusion(f32[768,512]{1,0:T(8,128)S(1)} %bitcast.33, s32[48]{0:T(128)S(1)} %fusion.16, bf16[48,512]{1,0:T(8,128)(2,1)S(1)} %bitcast.36), kind=kCustom, calls=%fused_computation.33 | custom fusion | flops 49152 | bytes 1622016 | tf_op jit(solution)/shard_map/scatter-add | solution.py:29
  60.9 3.3 %fusion.2 = bf16[768,512]{1,0:T(8,128)(2,1)} fusion(bf16[768,512]{1,0:T(8,128)(2,1)S(1)} %copy-done.7, bf16[512,512]{1,0:T(8,128)(2,1)} %param.16, f32[768,512]{1,0:T(8,128)S(1)} %scatter_custom_fusion.1, f32[768,512]{1,0:T(8,128)} %get-tuple-element.4, pred[768]{0:T(1024)(128)(4,1)S(1)} %iota_compare_fusion.3), kind=kOutput, calls=%fused_computation.11 | convolution fusion | flops 407764992 | bytes 5243648 | tf_op jit(solution)/shard_map/dot_general | solution.py:85
  64.2 2.0 %convolution_convert_fusion.1 = bf16[64,512]{1,0:T(8,128)(2,1)} fusion(bf16[512,512]{1,0:T(8,128)(2,1)} %param.17, f32[64,512]{1,0:T(8,128)} %reduce-scatter.2.cloned.1.call-done, f32[64,512]{1,0:T(8,128)S(1)} %copy-done.9), kind=kOutput, calls=%fused_computation.21 | convolution fusion | flops 33882112 | bytes 851968 | tf_op jit(solution)/shard_map/dot_general | solution.py:98
  (21 shorter events, 0.1 us)
Async XLA Ops:
  7.2 32.8 %copy-start = (bf16[512,512]{1,0:T(8,128)(2,1)S(1)}, bf16[512,512]{1,0:T(8,128)(2,1)}, u32[]{:S(2)}) copy-start(bf16[512,512]{1,0:T(8,128)(2,1)} %param.18) | copy-start | bytes 1572868
  7.2 11.6 %copy-start.1 = (s32[768,8]{0,1:T(8,128)S(1)}, s32[768,8]{0,1:T(8,128)}, u32[]{:S(2)}) copy-start(s32[768,8]{0,1:T(8,128)} %param.19) | copy-start | bytes 73732
  7.2 57.0 %reduce-scatter.2.cloned.1.call-start = ((), (), s32[]{:S(2)}) async-start(), calls=%async_computation.1 | async-start | bytes 393216 | tf_op jit(solution)/shard_map/reduce_scatter | solution.py:89
  18.8 1.1 %copy-start.4 = (bf16[768,512]{1,0:T(8,128)(2,1)S(1)}, bf16[768,512]{1,0:T(8,128)(2,1)}, u32[]{:S(2)}) copy-start(bf16[768,512]{1,0:T(8,128)(2,1)} %param.13) | copy-start | bytes 2359300
  18.8 1.3 %copy-start.8 = (bf16[512,512]{1,0:T(8,128)(2,1)S(1)}, bf16[512,512]{1,0:T(8,128)(2,1)}, u32[]{:S(2)}) copy-start(bf16[512,512]{1,0:T(8,128)(2,1)} %param.16) | copy-start | bytes 1572868
  20.1 17.6 %copy-start.3 = (s32[128]{0:T(128)S(1)}, s32[128]{0:T(128)}, u32[]{:S(2)}) copy-start(s32[128]{0:T(128)} %constant.58.clone) | copy-start | bytes 1540
  22.6 15.4 %copy-start.2 = (s32[768]{0:T(1024)S(1)}, s32[768]{0:T(1024)}, u32[]{:S(2)}) copy-start(s32[768]{0:T(1024)} %param.22) | copy-start | bytes 9220
  38.5 1.5 %copy-start.5 = (bf16[768,512]{1,0:T(8,128)(2,1)S(1)}, bf16[768,512]{1,0:T(8,128)(2,1)}, u32[]{:S(2)}) copy-start(bf16[768,512]{1,0:T(8,128)(2,1)} %param.13) | copy-start | bytes 2359300
  40.0 1.7 %copy-start.6 = (bf16[768,512]{1,0:T(8,128)(2,1)S(1)}, bf16[768,512]{1,0:T(8,128)(2,1)}, u32[]{:S(2)}) copy-start(bf16[768,512]{1,0:T(8,128)(2,1)} %param.15) | copy-start | bytes 2359300
  44.9 16.0 %copy-start.7 = (bf16[768,512]{1,0:T(8,128)(2,1)S(1)}, bf16[768,512]{1,0:T(8,128)(2,1)}, u32[]{:S(2)}) copy-start(bf16[768,512]{1,0:T(8,128)(2,1)} %param.15) | copy-start | bytes 2359300
  60.9 3.3 %copy-start.9 = (f32[64,512]{1,0:T(8,128)S(1)}, f32[64,512]{1,0:T(8,128)}, u32[]{:S(2)}) copy-start(f32[64,512]{1,0:T(8,128)} %get-tuple-element.6) | copy-start | bytes 393220
Sparse Core Ops, SparseCore 0:
  43.9 12.6 reduce-scatter.1
where the time goes:
time: 73.5 us; the launch traced here: 73.1 us
  blocking collectives  34.3 us (47%)
  between operations  14.9 us (20%)
  matrix products  14.1 us (19%)
  other arithmetic  5.19 us (7%)
  local copies, waits for them, and re-layouts  4.63 us (6%)
    all_gather x2, blocking collectives, trade_tiles(): everyone = lax.all_gather(tile_rows, 'dom', axis=0, tiled=True)  28.4 us
    all_gather x1, blocking collectives, on_device(): piece = lax.all_gather(coarse_msg, 'lvl', axis=0, tiled=True)  5.82 us
    dot_general x1, matrix products, on_device(): jnp.dot(d_pre_msg, jnp.transpose(w_message), preferred_element_type=jnp.f...  3.31 us
    scatter-add x2, other arithmetic, trade_tiles(): jnp.zeros((values.shape[0], values.shape[1]), jnp.float32).at[flat_index]  2.95 us
    dot_general x1, matrix products, on_device(): jnp.dot(d_pre_crs, jnp.transpose(w_coarse), preferred_element_type=jnp.fl...  2.03 us
    dot_general x1, matrix products, on_device(): jnp.dot(coarse_latents, w_coarse, preferred_element_type=jnp.float32)  1.95 us
    dot_general x1, matrix products, on_device(): jnp.dot(node_latents, w_message, preferred_element_type=jnp.float32)  1.87 us
    dot_general x1, matrix products, on_device(): pre_upd = jnp.dot(aggregate, w_update, preferred_element_type=jnp.float32)  1.72 us
  transfers between devices with their start and end apart: 1, of which 0 were waited for; matrix products, arithmetic and copies ran while one was open for 9% of the time, Pallas kernels for 0%

commit v1 on v0

v1 whole, which is shorter than its diff:
```python
import functools

import jax
import jax.numpy as jnp
from jax import lax
from jax.experimental import pallas as pl
from jax.experimental.pallas import tpu as pltpu
from jax.sharding import PartitionSpec as P

BLOCK = 128
MESH = pl.DeviceIdType.MESH


def gate(values):
    return 0.5 * jnp.tanh(0.5 * values) + 0.5


def dot(left, right, left_dim=1, right_dim=0):
    return lax.dot_general(
        left, right, (((left_dim,), (right_dim,)), ((), ())), preferred_element_type=jnp.float32
    )


def layer_kernel(
    n_dom,
    n_lvl,
    node_hbm,
    coarse_hbm,
    cot_hbm,
    w_message_hbm,
    w_coarse_hbm,
    w_update_hbm,
    words_hbm,
    tile_hbm,
    partner_hbm,
    assign_hbm,
    live_hbm,
    updated_hbm,
    d_nodes_hbm,
    d_coarse_hbm,
    node,
    coarse,
    cot,
    w_message,
    w_coarse,
    w_update,
    words,
    tile,
    partner,
    assign,
    live,
    adj_back,
    adj_fore,
    spread,
    gather,
    picker,
    pick_back,
    message,
    slope_msg,
    slope_crs,
    aggregate,
    d_agg,
    d_pre,
    updated,
    d_nodes,
    d_coarse,
    send_one,
    land_one,
    send_two,
    land_two,
    coarse_all,
    d_own,
    d_land,
    in_sem,
    out_sem,
    send_sem,
    one_sem,
    two_sem,
    crs_send_sem,
    crs_sem,
    grad_send_sem,
    grad_sem,
):
    rows, hidden = node.shape
    blocks = rows // BLOCK
    c_rows = coarse.shape[0]
    rounds, width = tile.shape
    tiles = n_dom * width
    me = lax.axis_index("dom")
    level = lax.axis_index("lvl")
    doms = [lax.rem(me + step, n_dom) for step in range(1, n_dom)]
    lvls = [lax.rem(level + step, n_lvl) for step in range(1, n_lvl)]

    barrier = pltpu.get_barrier_semaphore()
    for other in doms:
        pl.semaphore_signal(barrier, inc=1, device_id={"dom": other}, device_id_type=MESH)
    for other in lvls:
        pl.semaphore_signal(barrier, inc=1, device_id={"lvl": other}, device_id_type=MESH)

    pairs = dict(
        tile=(tile_hbm, tile),
        partner=(partner_hbm, partner),
        live=(live_hbm, live),
        node=(node_hbm, node),
        w_message=(w_message_hbm, w_message),
        coarse=(coarse_hbm, coarse),
        w_coarse=(w_coarse_hbm, w_coarse),
        words=(words_hbm, words),
        assign=(assign_hbm, assign),
        cot=(cot_hbm, cot),
        w_update=(w_update_hbm, w_update),
    )
    loads = {
        name: pltpu.make_async_copy(pair[0], pair[1], in_sem.at[i])
        for i, (name, pair) in enumerate(pairs.items())
    }
    for load in loads.values():
        load.start()

    def trade(source, landing, landing_sem, base):
        own = pl.ds(pl.multiple_of(me * width, width), width)
        copies = []
        for i, other in enumerate(doms):
            copy = pltpu.make_async_remote_copy(
                src_ref=source.at[pl.ds(pl.multiple_of(other * width, width), width)],
                dst_ref=landing.at[own],
                send_sem=send_sem.at[base + i],
                recv_sem=landing_sem.at[i],
                device_id={"dom": other},
                device_id_type=MESH,
            )
            copy.start()
            copies.append(copy)
        landing[own, :] = source[own, :]
        return copies

    loads["tile"].wait()
    loads["partner"].wait()
    loads["live"].wait()
    count = live[0]
    peer_of = lax.broadcasted_iota(jnp.int32, (1, tiles), 1) // width
    target = jnp.full((1, tiles), -1, jnp.int32)
    for r in range(rounds):
        wide = jnp.concatenate([tile[r : r + 1, :]] * n_dom, axis=1)
        target = jnp.where(peer_of == partner[r, me], wide, target)
    place = lax.broadcasted_iota(jnp.int32, (rows, tiles), 0)
    spread_f = jnp.where(place == target, 1.0, 0.0)
    spread[...] = spread_f.astype(jnp.bfloat16)
    gather_f = jnp.transpose(spread_f)
    gather[...] = gather_f.astype(jnp.bfloat16)
    lane = lax.broadcasted_iota(jnp.int32, (tiles, rows), 1)
    live_t = jnp.sum(jnp.where(lane < count, gather_f, 0.0), axis=1, keepdims=True)

    loads["node"].wait()
    loads["w_message"].wait()
    node_t = dot(gather[...], node[...]).astype(jnp.bfloat16)
    pre_t = dot(node_t, w_message[...])
    send_one[...] = (live_t * (pre_t * gate(pre_t))).astype(jnp.bfloat16)
    pl.semaphore_wait(barrier, n_dom - 1 + n_lvl - 1)
    sent = trade(send_one, land_one, one_sem, 0)

    loads["coarse"].wait()
    loads["w_coarse"].wait()
    pre_crs = dot(coarse[...], w_coarse[...])
    gate_crs = gate(pre_crs)
    silu_crs = pre_crs * gate_crs
    slope_crs[...] = gate_crs + silu_crs * (1.0 - gate_crs)
    own_crs = pl.ds(pl.multiple_of(level * c_rows, c_rows), c_rows)
    coarse_all[own_crs, :] = silu_crs.astype(jnp.bfloat16)
    crs_copies = []
    for i, other in enumerate(lvls):
        copy = pltpu.make_async_remote_copy(
            src_ref=coarse_all.at[own_crs],
            dst_ref=coarse_all.at[own_crs],
            send_sem=crs_send_sem.at[i],
            recv_sem=crs_sem.at[i],
            device_id={"lvl": other},
            device_id_type=MESH,
        )
        copy.start()
        crs_copies.append(copy)

    def live_rows(block):
        at = lax.broadcasted_iota(jnp.int32, (BLOCK, hidden), 0) + block * BLOCK
        return at < count

    for b in range(blocks):
        part = pl.ds(b * BLOCK, BLOCK)
        pre = dot(node[part, :], w_message[...])
        g = gate(pre)
        silu = pre * g
        alive = live_rows(b)
        message[part, :] = jnp.where(alive, silu, 0.0).astype(jnp.bfloat16)
        slope_msg[part, :] = jnp.where(alive, g + silu * (1.0 - g), 0.0)

    loads["words"].wait()
    loads["assign"].wait()
    bits = jnp.concatenate(
        [jnp.broadcast_to(words[w : w + 1, :], (16, rows)) for w in range(BLOCK // 16)], axis=0
    )
    shift = lax.broadcasted_iota(jnp.int32, (BLOCK, rows), 0) % 16
    bits = jnp.bitwise_and(jnp.right_shift(bits, shift), 1)
    adj_f = 0.125 * bits.astype(jnp.float32)
    adj_back[...] = adj_f.astype(jnp.bfloat16)
    adj_fore[...] = jnp.transpose(adj_f).astype(jnp.bfloat16)
    coarse_at = lax.broadcasted_iota(jnp.int32, (n_lvl * c_rows, rows), 0)
    pick_f = jnp.where(coarse_at == assign[...], 1.0, 0.0)
    pick_back[...] = pick_f.astype(jnp.bfloat16)
    picker[...] = jnp.transpose(pick_f).astype(jnp.bfloat16)
    loads["cot"].wait()
    cot_t = dot(gather[...], cot[...])

    for copy in sent:
        copy.wait_recv()
    for copy in crs_copies:
        copy.wait_recv()

    for b in range(blocks):
        part = pl.ds(b * BLOCK, BLOCK)
        total = dot(adj_fore[part, :], message[part, :])
        total += dot(spread[part, :], land_one[...])
        total += dot(picker[part, :], coarse_all[...])
        aggregate[part, :] = total.astype(jnp.bfloat16)

    loads["w_update"].wait()
    agg_t = dot(gather[...], aggregate[...]).astype(jnp.bfloat16)
    pre_t = dot(agg_t, w_update[...])
    g = gate(pre_t)
    d_t = (live_t * cot_t * (g * (1.0 + pre_t * (1.0 - g)))).astype(jnp.bfloat16)
    send_two[...] = dot(d_t, w_update[...], 1, 1).astype(jnp.bfloat16)
    sent_two = trade(send_two, land_two, two_sem, n_dom - 1)

    for b in range(blocks):
        part = pl.ds(b * BLOCK, BLOCK)
        pre = dot(aggregate[part, :], w_update[...])
        g = gate(pre)
        silu = pre * g
        alive = live_rows(b)
        slope = g + silu * (1.0 - g)
        updated[part, :] = (
            node[part, :].astype(jnp.float32) + jnp.where(alive, silu, 0.0)
        ).astype(jnp.bfloat16)
        d_pre[part, :] = jnp.where(alive, cot[part, :].astype(jnp.float32) * slope, 0.0).astype(
            jnp.bfloat16
        )
        d_agg[part, :] = dot(d_pre[part, :], w_update[...], 1, 1).astype(jnp.bfloat16)
    stores = [pltpu.make_async_copy(updated, updated_hbm, out_sem.at[0])]
    stores[0].start()

    d_own[...] = dot(pick_back[...], d_agg[...])
    grad_copies = []
    for i, other in enumerate(lvls):
        copy = pltpu.make_async_remote_copy(
            src_ref=d_own.at[pl.ds(pl.multiple_of(other * c_rows, c_rows), c_rows)],
            dst_ref=d_land.at[i],
            send_sem=grad_send_sem.at[i],
            recv_sem=grad_sem.at[i],
            device_id={"lvl": other},
            device_id_type=MESH,
        )
        copy.start()
        grad_copies.append(copy)

    for copy in sent_two:
        copy.wait_recv()
    for b in range(blocks):
        part = pl.ds(b * BLOCK, BLOCK)
        total = dot(adj_back[:, part], d_agg[part, :])
        total += dot(spread[part, :], land_two[...])
        d_pre_msg = (total * slope_msg[part, :]).astype(jnp.bfloat16)
        d_nodes[part, :] = (
            cot[part, :].astype(jnp.float32) + dot(d_pre_msg, w_message[...], 1, 1)
        ).astype(jnp.bfloat16)
    stores.append(pltpu.make_async_copy(d_nodes, d_nodes_hbm, out_sem.at[1]))
    stores[1].start()

    total = d_own[own_crs, :]
    for i, copy in enumerate(grad_copies):
        copy.wait_recv()
        total += d_land[i]
    d_pre_crs = (total * slope_crs[...]).astype(jnp.bfloat16)
    d_coarse[...] = dot(d_pre_crs, w_coarse[...], 1, 1).astype(jnp.bfloat16)
    stores.append(pltpu.make_async_copy(d_coarse, d_coarse_hbm, out_sem.at[2]))
    stores[2].start()

    for copy in sent + crs_copies + sent_two + grad_copies:
        copy.wait_send()
    for store in stores:
        store.wait()


def on_device(
    n_dom,
    n_lvl,
    node_latents,
    coarse_latents,
    cotangent,
    w_message,
    w_coarse,
    w_update,
    mask_words,
    tile_index,
    partner,
    assignment,
    live_counts,
):
    rows, hidden = node_latents.shape
    c_rows = coarse_latents.shape[0]
    rounds, width = tile_index.shape
    tiles = n_dom * width
    group = n_lvl * c_rows
    bf16, f32, i32 = jnp.bfloat16, jnp.float32, jnp.int32
    vmem = pltpu.VMEM
    dma = pltpu.SemaphoreType.DMA
    scratch = [
        vmem((rows, hidden), bf16),
        vmem((c_rows, hidden), bf16),
        vmem((rows, hidden), bf16),
        vmem((hidden, hidden), bf16),
        vmem((hidden, hidden), bf16),
        vmem((hidden, hidden), bf16),
        vmem((8, rows), i32),
        vmem((rounds, width), i32),
        pltpu.SMEM((rounds, n_dom), i32),
        vmem((1, rows), i32),
        pltpu.SMEM((1,), i32),
        vmem((BLOCK, rows), bf16),
        vmem((rows, BLOCK), bf16),
        vmem((rows, tiles), bf16),
        vmem((tiles, rows), bf16),
        vmem((rows, group), bf16),
        vmem((group, rows), bf16),
        vmem((rows, hidden), bf16),
        vmem((rows, hidden), f32),
        vmem((c_rows, hidden), f32),
        vmem((rows, hidden), bf16),
        vmem((rows, hidden), bf16),
        vmem((rows, hidden), bf16),
        vmem((rows, hidden), bf16),
        vmem((rows, hidden), bf16),
        vmem((c_rows, hidden), bf16),
        vmem((tiles, hidden), bf16),
        vmem((tiles, hidden), bf16),
        vmem((tiles, hidden), bf16),
        vmem((tiles, hidden), bf16),
        vmem((group, hidden), bf16),
        vmem((group, hidden), f32),
        vmem((n_lvl - 1, c_rows, hidden), f32),
        dma((11,)),
        dma((3,)),
        dma((2 * (n_dom - 1),)),
        dma((n_dom - 1,)),
        dma((n_dom - 1,)),
        dma((n_lvl - 1,)),
        dma((n_lvl - 1,)),
        dma((n_lvl - 1,)),
        dma((n_lvl - 1,)),
    ]
    anywhere = pl.BlockSpec(memory_space=pl.ANY)
    return pl.pallas_call(
        functools.partial(layer_kernel, n_dom, n_lvl),
        out_shape=(
            jax.ShapeDtypeStruct((rows, hidden), bf16),
            jax.ShapeDtypeStruct((rows, hidden), bf16),
            jax.ShapeDtypeStruct((c_rows, hidden), bf16),
        ),
        in_specs=[anywhere] * 11,
        out_specs=(anywhere,) * 3,
        scratch_shapes=scratch,
        compiler_params=pltpu.CompilerParams(
            collective_id=0, has_side_effects=True, vmem_limit_bytes=48 * 1024 * 1024
        ),
        name="layer",
    )(
        node_latents,
        coarse_latents,
        cotangent,
        w_message,
        w_coarse,
        w_update,
        jnp.transpose(mask_words),
        tile_index,
        partner,
        assignment.reshape(1, rows),
        live_counts,
    )


def solution(mesh):
    pieces = P(("grp", "dom", "lvl", "sub"), None)
    flat = P(("grp", "dom", "lvl", "sub"))
    return jax.shard_map(
        functools.partial(on_device, mesh.shape["dom"], mesh.shape["lvl"]),
        mesh=mesh,
        in_specs=(
            pieces,
            pieces,
            pieces,
            P(),
            P(),
            P(),
            pieces,
            pieces,
            P("grp", None),
            flat,
            flat,
        ),
        out_specs=(pieces, pieces, pieces),
        check_vma=False,
    )
```

time: 73.5 us -> 28.9 us (0.39)
  blocking collectives: 34.3 us -> 0 us
  Pallas kernels: 0 us -> 17 us
  matrix products: 14.1 us -> 0 us
  between operations: 14.9 us -> 1.32 us
  local copies, waits for them, and re-layouts: 4.63 us -> 10.1 us
  other arithmetic: 5.19 us -> 0 us
    all_gather x3 -> x0, blocking collectives: 34.3 us -> none  [the longest x2 28.4 us: trade_tiles(): everyone = lax.all_gather(tile_rows, 'dom', axis=0, tiled=True)]
    pallas_call x0 -> x1, Pallas kernels: none -> 17 us  [on_device(): pl.pallas_call(functools.partial(layer_kernel, n_dom, n_lvl), out_shape=(...]
    dot_general x10 -> x0, matrix products: 14.1 us -> none  [the longest x1 3.31 us: on_device(): jnp.dot(d_pre_msg, jnp.transpose(w_message), preferred_element_type=jnp.f...]
    unnamed x20 -> x21, local copies, waits for them, and re-layouts: 0.34 us -> 9.36 us
    gather x6 -> x0, local copies, waits for them, and re-layouts: 3.4 us -> none  [the longest x2 1.33 us: trade_tiles(): tile_rows = values[tile_index]]
    scatter-add x2 -> x0, other arithmetic: 2.95 us -> none  [trade_tiles(): jnp.zeros((values.shape[0], values.shape[1]), jnp.float32).at[flat_index]]
    select_n x3 -> x0, other arithmetic: 1.56 us -> none  [the longest x1 0.87 us: trade_tiles(): arrived = everyone[column * rounds + jnp.arange(rounds, dtype=jnp.int32)]]
  transfers between devices with their start and end apart: 1 -> 0, of which waited for: 0 -> 0; matrix products, arithmetic and copies ran while one was open for 9% -> 0% of each run, Pallas kernels for 0% -> 0%
where the time goes in v1:
time: 28.9 us; the launch traced here: 28.4 us
  Pallas kernels  17 us (59%)
  local copies, waits for them, and re-layouts  10.1 us (35%)
  between operations  1.32 us (5%)
    pallas_call x1, Pallas kernels, on_device(): pl.pallas_call(functools.partial(layer_kernel, n_dom, n_lvl), out_shape=(...  17 us
    unnamed x21, local copies, waits for them, and re-layouts  9.36 us
    reshape x1, local copies, waits for them, and re-layouts, on_device(): assignment.reshape(1, rows)  0.7 us

profile of v1, /device:TPU:0, one launch (start us, length us, event | category | flops | bytes accessed | tf_op | source)
XLA Modules:
  0.0 28.4 jit_solution(2784139439061906605)
XLA Ops:
  1.3 0.0 copy-start.7
  1.3 0.0 copy-start.8
  1.3 0.7 %reshape.9.assign_hbm = s32[1,768]{1,0:T(1,128)S(1)} reshape(s32[768]{0:T(1024)} %param.20) | data formatting | bytes 6144 | tf_op jit(solution)/shard_map/reshape | solution.py:384
  2.0 0.0 copy-done.7
  2.0 0.0 copy-done.8
  2.0 0.0 copy-start
  2.0 1.1 %copy-done = bf16[768,512]{1,0:T(8,128)(2,1)S(1)} copy-done((bf16[768,512]{1,0:T(8,128)(2,1)S(1)}, bf16[768,512]{1,0:T(8,128)(2,1)}, u32[]{:S(2)}) %copy-start) | copy-done | bytes 786456
  3.1 0.0 copy-start.1
  3.1 1.1 %copy-done.1 = bf16[768,512]{1,0:T(8,128)(2,1)S(1)} copy-done((bf16[768,512]{1,0:T(8,128)(2,1)S(1)}, bf16[768,512]{1,0:T(8,128)(2,1)}, u32[]{:S(2)}) %copy-start.1) | copy-done | bytes 786456
  4.3 0.0 copy-start.2
  4.3 1.0 %copy-done.2 = bf16[512,512]{1,0:T(8,128)(2,1)S(1)} copy-done((bf16[512,512]{1,0:T(8,128)(2,1)S(1)}, bf16[512,512]{1,0:T(8,128)(2,1)}, u32[]{:S(2)}) %copy-start.2) | copy-done | bytes 524312
  5.3 0.0 copy-start.3
  5.3 1.0 %copy-done.3 = bf16[512,512]{1,0:T(8,128)(2,1)S(1)} copy-done((bf16[512,512]{1,0:T(8,128)(2,1)S(1)}, bf16[512,512]{1,0:T(8,128)(2,1)}, u32[]{:S(2)}) %copy-start.3) | copy-done | bytes 524312
  6.4 0.0 copy-start.4
  6.4 1.0 %copy-done.4 = bf16[512,512]{1,0:T(8,128)(2,1)S(1)} copy-done((bf16[512,512]{1,0:T(8,128)(2,1)S(1)}, bf16[512,512]{1,0:T(8,128)(2,1)}, u32[]{:S(2)}) %copy-start.4) | copy-done | bytes 524312
  7.4 0.0 copy-start.5
  7.4 0.8 %copy-done.5 = bf16[64,512]{1,0:T(8,128)(2,1)S(1)} copy-done((bf16[64,512]{1,0:T(8,128)(2,1)S(1)}, bf16[64,512]{1,0:T(8,128)(2,1)}, u32[]{:S(2)}) %copy-start.5) | copy-done | bytes 65560
  8.2 0.0 copy-start.6
  8.2 0.7 %copy-done.6 = s32[768,8]{0,1:T(8,128)S(1)} copy-done((s32[768,8]{0,1:T(8,128)S(1)}, s32[768,8]{0,1:T(8,128)}, u32[]{:S(2)}) %copy-start.6) | copy-done | bytes 24600
  9.0 17.0 %layer.1 = (bf16[768,512]{1,0:T(8,128)(2,1)S(1)}, bf16[768,512]{1,0:T(8,128)(2,1)S(1)}, bf16[64,512]{1,0:T(8,128)(2,1)S(1)}) custom-call(bf16[768,512]{1,0:T(8,128)(2,1)S(1)} %copy-done, bf16[64,512]{1,0:T(8,128)(2,1)S(1)} %copy-done.5, bf16[768,512]{1,0:T(8,128)(2,1)S(1)} %copy-done.1, bf16[512,512]{1,0:T(8,128)(2,1)S(1)} %copy-done.2, ...), custom_call_target="tpu_custom_call" | custom-call | tf_op jit(solution)/shard_map/layer/pallas_call | solution.py:360
  26.0 0.9 %copy.18 = bf16[768,512]{1,0:T(8,128)(2,1)} copy(bf16[768,512]{1,0:T(8,128)(2,1)S(1)} %get-tuple-element.6) | data formatting | bytes 1572864
  26.9 0.9 %copy.19 = bf16[768,512]{1,0:T(8,128)(2,1)} copy(bf16[768,512]{1,0:T(8,128)(2,1)S(1)} %get-tuple-element.7) | data formatting | bytes 1572864
  27.7 0.6 %copy.20 = bf16[64,512]{1,0:T(8,128)(2,1)} copy(bf16[64,512]{1,0:T(8,128)(2,1)S(1)} %get-tuple-element.8) | data formatting | bytes 131072
Async XLA Ops:
  1.3 0.7 %copy-start.7 = (s32[3,16]{1,0:T(4,128)S(1)}, s32[3,16]{1,0:T(4,128)}, u32[]{:S(2)}) copy-start(s32[3,16]{1,0:T(4,128)} %tile_hbm.1) | copy-start | bytes 580
  1.3 0.7 %copy-start.8 = (s32[3,4]{1,0:T(4,128)S(1)}, s32[3,4]{1,0:T(4,128)}, u32[]{:S(2)}) copy-start(s32[3,4]{1,0:T(4,128)} %partner_hbm.1) | copy-start | bytes 148
  2.0 1.1 %copy-start = (bf16[768,512]{1,0:T(8,128)(2,1)S(1)}, bf16[768,512]{1,0:T(8,128)(2,1)}, u32[]{:S(2)}) copy-start(bf16[768,512]{1,0:T(8,128)(2,1)} %node_hbm.1) | copy-start | bytes 2359300
  3.1 1.1 %copy-start.1 = (bf16[768,512]{1,0:T(8,128)(2,1)S(1)}, bf16[768,512]{1,0:T(8,128)(2,1)}, u32[]{:S(2)}) copy-start(bf16[768,512]{1,0:T(8,128)(2,1)} %cot_hbm.1) | copy-start | bytes 2359300
  4.3 1.0 %copy-start.2 = (bf16[512,512]{1,0:T(8,128)(2,1)S(1)}, bf16[512,512]{1,0:T(8,128)(2,1)}, u32[]{:S(2)}) copy-start(bf16[512,512]{1,0:T(8,128)(2,1)} %w_message_hbm.1) | copy-start | bytes 1572868
  5.3 1.0 %copy-start.3 = (bf16[512,512]{1,0:T(8,128)(2,1)S(1)}, bf16[512,512]{1,0:T(8,128)(2,1)}, u32[]{:S(2)}) copy-start(bf16[512,512]{1,0:T(8,128)(2,1)} %w_coarse_hbm.1) | copy-start | bytes 1572868
  6.4 1.0 %copy-start.4 = (bf16[512,512]{1,0:T(8,128)(2,1)S(1)}, bf16[512,512]{1,0:T(8,128)(2,1)}, u32[]{:S(2)}) copy-start(bf16[512,512]{1,0:T(8,128)(2,1)} %w_update_hbm.1) | copy-start | bytes 1572868
  7.4 0.8 %copy-start.5 = (bf16[64,512]{1,0:T(8,128)(2,1)S(1)}, bf16[64,512]{1,0:T(8,128)(2,1)}, u32[]{:S(2)}) copy-start(bf16[64,512]{1,0:T(8,128)(2,1)} %coarse_hbm.1) | copy-start | bytes 196612
  8.2 0.7 %copy-start.6 = (s32[768,8]{0,1:T(8,128)S(1)}, s32[768,8]{0,1:T(8,128)}, u32[]{:S(2)}) copy-start(s32[768,8]{0,1:T(8,128)} %param.17) | copy-start | bytes 73732

commit v2 on v1

--- a/solution.py
+++ b/solution.py
@@ -204,7 +204,7 @@
     adj_back[...] = adj_f.astype(jnp.bfloat16)
     adj_fore[...] = jnp.transpose(adj_f).astype(jnp.bfloat16)
     coarse_at = lax.broadcasted_iota(jnp.int32, (n_lvl * c_rows, rows), 0)
-    pick_f = jnp.where(coarse_at == assign[...], 1.0, 0.0)
+    pick_f = jnp.where(coarse_at == assign[...].reshape(1, rows), 1.0, 0.0)
     pick_back[...] = pick_f.astype(jnp.bfloat16)
     picker[...] = jnp.transpose(pick_f).astype(jnp.bfloat16)
     loads["cot"].wait()
@@ -244,6 +244,7 @@
             jnp.bfloat16
         )
         d_agg[part, :] = dot(d_pre[part, :], w_update[...], 1, 1).astype(jnp.bfloat16)
+
     stores = [pltpu.make_async_copy(updated, updated_hbm, out_sem.at[0])]
     stores[0].start()
 
@@ -271,6 +272,7 @@
         d_nodes[part, :] = (
             cot[part, :].astype(jnp.float32) + dot(d_pre_msg, w_message[...], 1, 1)
         ).astype(jnp.bfloat16)
+
     stores.append(pltpu.make_async_copy(d_nodes, d_nodes_hbm, out_sem.at[1]))
     stores[1].start()
 
@@ -280,11 +282,36 @@
         total += d_land[i]
     d_pre_crs = (total * slope_crs[...]).astype(jnp.bfloat16)
     d_coarse[...] = dot(d_pre_crs, w_coarse[...], 1, 1).astype(jnp.bfloat16)
+
     stores.append(pltpu.make_async_copy(d_coarse, d_coarse_hbm, out_sem.at[2]))
     stores[2].start()
-
     for copy in sent + crs_copies + sent_two + grad_copies:
         copy.wait_send()
+    for store in stores:
+        store.wait()
+
+
+def store_kernel(updated, d_nodes, d_coarse, *refs):
+    outs, stages, in_sem, out_sem = refs[:3], refs[3:6], refs[6], refs[7]
+    parts = []
+    for i, ref in enumerate((updated, d_nodes, d_coarse)):
+        rows = ref.shape[0]
+        step = min(rows, 256)
+        parts += [(i, pl.ds(start, step)) for start in range(0, rows, step)]
+    sources = (updated, d_nodes, d_coarse)
+    loads = [
+        pltpu.make_async_copy(sources[i].at[at], stages[i].at[at], in_sem.at[n])
+        for n, (i, at) in enumerate(parts)
+    ]
+    stores = [
+        pltpu.make_async_copy(stages[i].at[at], outs[i].at[at], out_sem.at[n])
+        for n, (i, at) in enumerate(parts)
+    ]
+    for load in loads:
+        load.start()
+    for load, store in zip(loads, stores):
+        load.wait()
+        store.start()
     for store in stores:
         store.wait()
 
@@ -322,7 +349,7 @@
         vmem((8, rows), i32),
         vmem((rounds, width), i32),
         pltpu.SMEM((rounds, n_dom), i32),
-        vmem((1, rows), i32),
+        vmem((rows,), i32),
         pltpu.SMEM((1,), i32),
         vmem((BLOCK, rows), bf16),
         vmem((rows, BLOCK), bf16),
@@ -356,19 +383,20 @@
         dma((n_lvl - 1,)),
         dma((n_lvl - 1,)),
     ]
-    anywhere = pl.BlockSpec(memory_space=pl.ANY)
-    return pl.pallas_call(
+    far = pl.BlockSpec(memory_space=pl.ANY)
+    outs = (
+        jax.ShapeDtypeStruct((rows, hidden), bf16),
+        jax.ShapeDtypeStruct((rows, hidden), bf16),
+        jax.ShapeDtypeStruct((c_rows, hidden), bf16),
+    )
+    results = pl.pallas_call(
         functools.partial(layer_kernel, n_dom, n_lvl),
-        out_shape=(
-            jax.ShapeDtypeStruct((rows, hidden), bf16),
-            jax.ShapeDtypeStruct((rows, hidden), bf16),
-            jax.ShapeDtypeStruct((c_rows, hidden), bf16),
-        ),
-        in_specs=[anywhere] * 11,
-        out_specs=(anywhere,) * 3,
+        out_shape=outs,
+        in_specs=[far] * 11,
+        out_specs=(far,) * 3,
         scratch_shapes=scratch,
         compiler_params=pltpu.CompilerParams(
-            collective_id=0, has_side_effects=True, vmem_limit_bytes=48 * 1024 * 1024
+            collective_id=0, has_side_effects=True, vmem_limit_bytes=56 * 1024 * 1024
         ),
         name="layer",
     )(
@@ -381,9 +409,18 @@
         jnp.transpose(mask_words),
         tile_index,
         partner,
-        assignment.reshape(1, rows),
+        assignment,
         live_counts,
     )
+    return pl.pallas_call(
+        store_kernel,
+        out_shape=outs,
+        in_specs=[far] * 3,
+        out_specs=(far,) * 3,
+        scratch_shapes=[vmem(out.shape, bf16) for out in outs] + [dma((7,)), dma((7,))],
+        compiler_params=pltpu.CompilerParams(vmem_limit_bytes=56 * 1024 * 1024),
+        name="store",
+    )(*results)
 
 
 def solution(mesh):

time: 28.9 us -> 21.5 us (0.74); the launches traced: 28.4 us -> 21.4 us
  local copies, waits for them, and re-layouts: 10.1 us -> 0 us
  Pallas kernels: 17 us -> 20.1 us
    unnamed x21 -> x0, local copies, waits for them, and re-layouts: 9.36 us -> none
    pallas_call x1 -> x2, Pallas kernels: 17 us -> 20.1 us  [the longest x1 17.9 us: on_device(): pl.pallas_call(functools.partial(layer_kernel, n_dom, n_lvl), out_shape=o...]
    reshape x1 -> x0, local copies, waits for them, and re-layouts: 0.7 us -> none  [on_device(): assignment.reshape(1, rows)]
where the time goes in v2:
time: 21.5 us; the launch traced here: 21.4 us
  Pallas kernels  20.1 us (93%)
  between operations  1.29 us (6%)
    pallas_call x1, Pallas kernels, on_device(): pl.pallas_call(functools.partial(layer_kernel, n_dom, n_lvl), out_shape=o...  17.9 us
    pallas_call x1, Pallas kernels, on_device(): pl.pallas_call(store_kernel, out_shape=outs, in_specs=[far] * 3, out_spec...  2.22 us

profile of v2, /device:TPU:0, one launch (start us, length us, event | category | flops | bytes accessed | tf_op | source)
XLA Modules:
  0.0 21.4 jit_solution(12874535513542989337)
XLA Ops:
  1.3 17.9 %layer.1 = (bf16[768,512]{1,0:T(8,128)(2,1)}, bf16[768,512]{1,0:T(8,128)(2,1)}, bf16[64,512]{1,0:T(8,128)(2,1)}) custom-call(bf16[768,512]{1,0:T(8,128)(2,1)} %node_hbm.1, bf16[64,512]{1,0:T(8,128)(2,1)} %coarse_hbm.1, bf16[768,512]{1,0:T(8,128)(2,1)} %cot_hbm.1, bf16[512,512]{1,0:T(8,128)(2,1)} %w_message_hbm.1, bf16[512,512]{1,0:T(8,128)(2,1)} %w_coarse_hbm.1, ...), custom_call_target="tpu_custom_call" | custom-call | tf_op jit(solution)/shard_map/layer/pallas_call | solution.py:392
  19.1 2.2 %store.1 = (bf16[768,512]{1,0:T(8,128)(2,1)}, bf16[768,512]{1,0:T(8,128)(2,1)}, bf16[64,512]{1,0:T(8,128)(2,1)}) custom-call(bf16[768,512]{1,0:T(8,128)(2,1)} %get-tuple-element.6.updated, bf16[768,512]{1,0:T(8,128)(2,1)} %get-tuple-element.7.d_nodes, bf16[64,512]{1,0:T(8,128)(2,1)} %get-tuple-element.8.d_coarse), custom_call_target="tpu_custom_call" | custom-call | tf_op jit(solution)/shard_map/store/pallas_call | solution.py:415

commit v3 on v2

--- a/solution.py
+++ b/solution.py
@@ -8,6 +8,7 @@
 from jax.sharding import PartitionSpec as P
 
 BLOCK = 128
+STEP = 384
 MESH = pl.DeviceIdType.MESH
 
 
@@ -53,6 +54,9 @@
     adj_fore,
     spread,
     gather,
+    reach,
+    echo,
+    reach_crs,
     picker,
     pick_back,
     message,
@@ -70,6 +74,7 @@
     land_two,
     coarse_all,
     d_own,
+    d_send,
     d_land,
     in_sem,
     out_sem,
@@ -101,14 +106,14 @@
         tile=(tile_hbm, tile),
         partner=(partner_hbm, partner),
         live=(live_hbm, live),
+        words=(words_hbm, words),
+        assign=(assign_hbm, assign),
         node=(node_hbm, node),
         w_message=(w_message_hbm, w_message),
         coarse=(coarse_hbm, coarse),
         w_coarse=(w_coarse_hbm, w_coarse),
-        words=(words_hbm, words),
-        assign=(assign_hbm, assign),
+        w_update=(w_update_hbm, w_update),
         cot=(cot_hbm, cot),
-        w_update=(w_update_hbm, w_update),
     )
     loads = {
         name: pltpu.make_async_copy(pair[0], pair[1], in_sem.at[i])
@@ -150,6 +155,26 @@
     gather[...] = gather_f.astype(jnp.bfloat16)
     lane = lax.broadcasted_iota(jnp.int32, (tiles, rows), 1)
     live_t = jnp.sum(jnp.where(lane < count, gather_f, 0.0), axis=1, keepdims=True)
+
+    loads["words"].wait()
+    loads["assign"].wait()
+    bits = jnp.concatenate(
+        [jnp.broadcast_to(words[w : w + 1, :], (16, rows)) for w in range(BLOCK // 16)], axis=0
+    )
+    shift = lax.broadcasted_iota(jnp.int32, (BLOCK, rows), 0) % 16
+    bits = jnp.bitwise_and(jnp.right_shift(bits, shift), 1)
+    adj_f = 0.125 * bits.astype(jnp.float32)
+    adj_back[...] = adj_f.astype(jnp.bfloat16)
+    adj_fore[...] = jnp.transpose(adj_f).astype(jnp.bfloat16)
+    coarse_at = lax.broadcasted_iota(jnp.int32, (n_lvl * c_rows, rows), 0)
+    pick_f = jnp.where(coarse_at == assign[...].reshape(1, rows), 1.0, 0.0)
+    pick_back[...] = pick_f.astype(jnp.bfloat16)
+    picker[...] = jnp.transpose(pick_f).astype(jnp.bfloat16)
+    for b in range(blocks):
+        part = pl.ds(b * BLOCK, BLOCK)
+        reach[:, part] = dot(gather[:, part], adj_fore[part, :]).astype(jnp.bfloat16)
+    echo[...] = dot(gather[...], spread[...]).astype(jnp.bfloat16)
+    reach_crs[...] = dot(gather[...], picker[...]).astype(jnp.bfloat16)
 
     loads["node"].wait()
     loads["w_message"].wait()
@@ -180,33 +205,19 @@
         copy.start()
         crs_copies.append(copy)
 
-    def live_rows(block):
-        at = lax.broadcasted_iota(jnp.int32, (BLOCK, hidden), 0) + block * BLOCK
+    def live_rows(start):
+        at = lax.broadcasted_iota(jnp.int32, (STEP, hidden), 0) + start
         return at < count
 
-    for b in range(blocks):
-        part = pl.ds(b * BLOCK, BLOCK)
+    for start in range(0, rows, STEP):
+        part = pl.ds(start, STEP)
         pre = dot(node[part, :], w_message[...])
         g = gate(pre)
         silu = pre * g
-        alive = live_rows(b)
+        alive = live_rows(start)
         message[part, :] = jnp.where(alive, silu, 0.0).astype(jnp.bfloat16)
         slope_msg[part, :] = jnp.where(alive, g + silu * (1.0 - g), 0.0)
 
-    loads["words"].wait()
-    loads["assign"].wait()
-    bits = jnp.concatenate(
-        [jnp.broadcast_to(words[w : w + 1, :], (16, rows)) for w in range(BLOCK // 16)], axis=0
-    )
-    shift = lax.broadcasted_iota(jnp.int32, (BLOCK, rows), 0) % 16
-    bits = jnp.bitwise_and(jnp.right_shift(bits, shift), 1)
-    adj_f = 0.125 * bits.astype(jnp.float32)
-    adj_back[...] = adj_f.astype(jnp.bfloat16)
-    adj_fore[...] = jnp.transpose(adj_f).astype(jnp.bfloat16)
-    coarse_at = lax.broadcasted_iota(jnp.int32, (n_lvl * c_rows, rows), 0)
-    pick_f = jnp.where(coarse_at == assign[...].reshape(1, rows), 1.0, 0.0)
-    pick_back[...] = pick_f.astype(jnp.bfloat16)
-    picker[...] = jnp.transpose(pick_f).astype(jnp.bfloat16)
     loads["cot"].wait()
     cot_t = dot(gather[...], cot[...])
 
@@ -214,6 +225,16 @@
         copy.wait_recv()
     for copy in crs_copies:
         copy.wait_recv()
+
+    loads["w_update"].wait()
+    agg_t = dot(reach[...], message[...])
+    agg_t += dot(reach_crs[...], coarse_all[...])
+    agg_t = (agg_t + dot(echo[...], land_one[...])).astype(jnp.bfloat16)
+    pre_t = dot(agg_t, w_update[...])
+    g = gate(pre_t)
+    d_t = (live_t * cot_t * (g * (1.0 + pre_t * (1.0 - g)))).astype(jnp.bfloat16)
+    send_two[...] = dot(d_t, w_update[...], 1, 1).astype(jnp.bfloat16)
+    sent_two = trade(send_two, land_two, two_sem, n_dom - 1)
 
     for b in range(blocks):
         part = pl.ds(b * BLOCK, BLOCK)
@@ -222,20 +243,12 @@
         total += dot(picker[part, :], coarse_all[...])
         aggregate[part, :] = total.astype(jnp.bfloat16)
 
-    loads["w_update"].wait()
-    agg_t = dot(gather[...], aggregate[...]).astype(jnp.bfloat16)
-    pre_t = dot(agg_t, w_update[...])
-    g = gate(pre_t)
-    d_t = (live_t * cot_t * (g * (1.0 + pre_t * (1.0 - g)))).astype(jnp.bfloat16)
-    send_two[...] = dot(d_t, w_update[...], 1, 1).astype(jnp.bfloat16)
-    sent_two = trade(send_two, land_two, two_sem, n_dom - 1)
-
-    for b in range(blocks):
-        part = pl.ds(b * BLOCK, BLOCK)
+    for start in range(0, rows, STEP):
+        part = pl.ds(start, STEP)
         pre = dot(aggregate[part, :], w_update[...])
         g = gate(pre)
         silu = pre * g
-        alive = live_rows(b)
+        alive = live_rows(start)
         slope = g + silu * (1.0 - g)
         updated[part, :] = (
             node[part, :].astype(jnp.float32) + jnp.where(alive, silu, 0.0)
@@ -249,10 +262,11 @@
     stores[0].start()
 
     d_own[...] = dot(pick_back[...], d_agg[...])
+    d_send[...] = d_own[...].astype(jnp.bfloat16)
     grad_copies = []
     for i, other in enumerate(lvls):
         copy = pltpu.make_async_remote_copy(
-            src_ref=d_own.at[pl.ds(pl.multiple_of(other * c_rows, c_rows), c_rows)],
+            src_ref=d_send.at[pl.ds(pl.multiple_of(other * c_rows, c_rows), c_rows)],
             dst_ref=d_land.at[i],
             send_sem=grad_send_sem.at[i],
             recv_sem=grad_sem.at[i],
@@ -264,27 +278,32 @@
 
     for copy in sent_two:
         copy.wait_recv()
-    for b in range(blocks):
-        part = pl.ds(b * BLOCK, BLOCK)
-        total = dot(adj_back[:, part], d_agg[part, :])
-        total += dot(spread[part, :], land_two[...])
-        d_pre_msg = (total * slope_msg[part, :]).astype(jnp.bfloat16)
+    for start in range(0, rows, STEP):
+        for b in range(start // BLOCK, (start + STEP) // BLOCK):
+            part = pl.ds(b * BLOCK, BLOCK)
+            total = dot(adj_back[:, part], d_agg[part, :])
+            total += dot(spread[part, :], land_two[...])
+            d_pre[part, :] = (total * slope_msg[part, :]).astype(jnp.bfloat16)
+        part = pl.ds(start, STEP)
         d_nodes[part, :] = (
-            cot[part, :].astype(jnp.float32) + dot(d_pre_msg, w_message[...], 1, 1)
+            cot[part, :].astype(jnp.float32) + dot(d_pre[part, :], w_message[...], 1, 1)
         ).astype(jnp.bfloat16)
-
-    stores.append(pltpu.make_async_copy(d_nodes, d_nodes_hbm, out_sem.at[1]))
-    stores[1].start()
+        stores.append(
+            pltpu.make_async_copy(
+                d_nodes.at[part], d_nodes_hbm.at[part], out_sem.at[2 + start // STEP]
+            )
+        )
+        stores[-1].start()
 
     total = d_own[own_crs, :]
     for i, copy in enumerate(grad_copies):
         copy.wait_recv()
-        total += d_land[i]
+        total += d_land[i].astype(jnp.float32)
     d_pre_crs = (total * slope_crs[...]).astype(jnp.bfloat16)
     d_coarse[...] = dot(d_pre_crs, w_coarse[...], 1, 1).astype(jnp.bfloat16)
 
-    stores.append(pltpu.make_async_copy(d_coarse, d_coarse_hbm, out_sem.at[2]))
-    stores[2].start()
+    stores.append(pltpu.make_async_copy(d_coarse, d_coarse_hbm, out_sem.at[1]))
+    stores[-1].start()
     for copy in sent + crs_copies + sent_two + grad_copies:
         copy.wait_send()
     for store in stores:
@@ -355,6 +374,9 @@
         vmem((rows, BLOCK), bf16),
         vmem((rows, tiles), bf16),
         vmem((tiles, rows), bf16),
+        vmem((tiles, rows), bf16),
+        vmem((tiles, tiles), bf16),
+        vmem((tiles, group), bf16),
         vmem((rows, group), bf16),
         vmem((group, rows), bf16),
         vmem((rows, hidden), bf16),
@@ -372,9 +394,10 @@
         vmem((tiles, hidden), bf16),
         vmem((group, hidden), bf16),
         vmem((group, hidden), f32),
-        vmem((n_lvl - 1, c_rows, hidden), f32),
+        vmem((group, hidden), bf16),
+        vmem((n_lvl - 1, c_rows, hidden), bf16),
         dma((11,)),
-        dma((3,)),
+        dma((2 + rows // STEP,)),
         dma((2 * (n_dom - 1),)),
         dma((n_dom - 1,)),
         dma((n_dom - 1,)),

time: 21.5 us -> 20.5 us (0.953)
  Pallas kernels: 20.1 us -> 19 us
    pallas_call x1, Pallas kernels: 17.9 us -> 16.8 us  [on_device(): pl.pallas_call(functools.partial(layer_kernel, n_dom, n_lvl), out_shape=o...]
where the time goes in v3:
time: 20.5 us; the launch traced here: 20.3 us
  Pallas kernels  19 us (93%)
  between operations  1.29 us (6%)
    pallas_call x1, Pallas kernels, on_device(): pl.pallas_call(functools.partial(layer_kernel, n_dom, n_lvl), out_shape=o...  16.8 us
    pallas_call x1, Pallas kernels, on_device(): pl.pallas_call(store_kernel, out_shape=outs, in_specs=[far] * 3, out_spec...  2.22 us

profile of v3, /device:TPU:0, one launch (start us, length us, event | category | flops | bytes accessed | tf_op | source)
XLA Modules:
  0.0 20.3 jit_solution(9272800262936804741)
XLA Ops:
  1.3 16.8 %layer.1 = (bf16[768,512]{1,0:T(8,128)(2,1)}, bf16[768,512]{1,0:T(8,128)(2,1)}, bf16[64,512]{1,0:T(8,128)(2,1)}) custom-call(bf16[768,512]{1,0:T(8,128)(2,1)} %node_hbm.1, bf16[64,512]{1,0:T(8,128)(2,1)} %coarse_hbm.1, bf16[768,512]{1,0:T(8,128)(2,1)} %cot_hbm.1, bf16[512,512]{1,0:T(8,128)(2,1)} %w_message_hbm.1, bf16[512,512]{1,0:T(8,128)(2,1)} %w_coarse_hbm.1, ...), custom_call_target="tpu_custom_call" | custom-call | tf_op jit(solution)/shard_map/layer/pallas_call | solution.py:415
  18.1 2.2 %store.1 = (bf16[768,512]{1,0:T(8,128)(2,1)}, bf16[768,512]{1,0:T(8,128)(2,1)}, bf16[64,512]{1,0:T(8,128)(2,1)}) custom-call(bf16[768,512]{1,0:T(8,128)(2,1)} %get-tuple-element.6.updated, bf16[768,512]{1,0:T(8,128)(2,1)} %get-tuple-element.7.d_nodes, bf16[64,512]{1,0:T(8,128)(2,1)} %get-tuple-element.8.d_coarse), custom_call_target="tpu_custom_call" | custom-call | tf_op jit(solution)/shard_map/store/pallas_call | solution.py:438

commit v4 on v3

--- a/solution.py
+++ b/solution.py
@@ -55,13 +55,13 @@
     spread,
     gather,
     reach,
-    echo,
-    reach_crs,
-    picker,
+    reach_far,
+    far_fore,
     pick_back,
     message,
     slope_msg,
     slope_crs,
+    near,
     aggregate,
     d_agg,
     d_pre,
@@ -69,10 +69,9 @@
     d_nodes,
     d_coarse,
     send_one,
-    land_one,
     send_two,
     land_two,
-    coarse_all,
+    landed,
     d_own,
     d_send,
     d_land,
@@ -156,6 +155,36 @@
     lane = lax.broadcasted_iota(jnp.int32, (tiles, rows), 1)
     live_t = jnp.sum(jnp.where(lane < count, gather_f, 0.0), axis=1, keepdims=True)
 
+    loads["node"].wait()
+    loads["w_message"].wait()
+    node_t = dot(gather[...], node[...]).astype(jnp.bfloat16)
+    pre_t = dot(node_t, w_message[...])
+    send_one[...] = (live_t * (pre_t * gate(pre_t))).astype(jnp.bfloat16)
+    pl.semaphore_wait(barrier, n_dom - 1 + n_lvl - 1)
+    sent = trade(send_one, landed, one_sem, 0)
+
+    loads["coarse"].wait()
+    loads["w_coarse"].wait()
+    pre_crs = dot(coarse[...], w_coarse[...])
+    gate_crs = gate(pre_crs)
+    silu_crs = pre_crs * gate_crs
+    slope_crs[...] = gate_crs + silu_crs * (1.0 - gate_crs)
+    own_crs = pl.ds(pl.multiple_of(level * c_rows, c_rows), c_rows)
+    own_far = pl.ds(pl.multiple_of(tiles + level * c_rows, c_rows), c_rows)
+    landed[own_far, :] = silu_crs.astype(jnp.bfloat16)
+    crs_copies = []
+    for i, other in enumerate(lvls):
+        copy = pltpu.make_async_remote_copy(
+            src_ref=landed.at[own_far],
+            dst_ref=landed.at[own_far],
+            send_sem=crs_send_sem.at[i],
+            recv_sem=crs_sem.at[i],
+            device_id={"lvl": other},
+            device_id_type=MESH,
+        )
+        copy.start()
+        crs_copies.append(copy)
+
     loads["words"].wait()
     loads["assign"].wait()
     bits = jnp.concatenate(
@@ -169,41 +198,11 @@
     coarse_at = lax.broadcasted_iota(jnp.int32, (n_lvl * c_rows, rows), 0)
     pick_f = jnp.where(coarse_at == assign[...].reshape(1, rows), 1.0, 0.0)
     pick_back[...] = pick_f.astype(jnp.bfloat16)
-    picker[...] = jnp.transpose(pick_f).astype(jnp.bfloat16)
+    far_fore[...] = jnp.concatenate([spread_f, jnp.transpose(pick_f)], axis=1).astype(jnp.bfloat16)
     for b in range(blocks):
         part = pl.ds(b * BLOCK, BLOCK)
         reach[:, part] = dot(gather[:, part], adj_fore[part, :]).astype(jnp.bfloat16)
-    echo[...] = dot(gather[...], spread[...]).astype(jnp.bfloat16)
-    reach_crs[...] = dot(gather[...], picker[...]).astype(jnp.bfloat16)
-
-    loads["node"].wait()
-    loads["w_message"].wait()
-    node_t = dot(gather[...], node[...]).astype(jnp.bfloat16)
-    pre_t = dot(node_t, w_message[...])
-    send_one[...] = (live_t * (pre_t * gate(pre_t))).astype(jnp.bfloat16)
-    pl.semaphore_wait(barrier, n_dom - 1 + n_lvl - 1)
-    sent = trade(send_one, land_one, one_sem, 0)
-
-    loads["coarse"].wait()
-    loads["w_coarse"].wait()
-    pre_crs = dot(coarse[...], w_coarse[...])
-    gate_crs = gate(pre_crs)
-    silu_crs = pre_crs * gate_crs
-    slope_crs[...] = gate_crs + silu_crs * (1.0 - gate_crs)
-    own_crs = pl.ds(pl.multiple_of(level * c_rows, c_rows), c_rows)
-    coarse_all[own_crs, :] = silu_crs.astype(jnp.bfloat16)
-    crs_copies = []
-    for i, other in enumerate(lvls):
-        copy = pltpu.make_async_remote_copy(
-            src_ref=coarse_all.at[own_crs],
-            dst_ref=coarse_all.at[own_crs],
-            send_sem=crs_send_sem.at[i],
-            recv_sem=crs_sem.at[i],
-            device_id={"lvl": other},
-            device_id_type=MESH,
-        )
-        copy.start()
-        crs_copies.append(copy)
+    reach_far[...] = dot(gather[...], far_fore[...]).astype(jnp.bfloat16)
 
     def live_rows(start):
         at = lax.broadcasted_iota(jnp.int32, (STEP, hidden), 0) + start
@@ -221,6 +220,9 @@
     loads["cot"].wait()
     cot_t = dot(gather[...], cot[...])
 
+    for b in range(blocks):
+        part = pl.ds(b * BLOCK, BLOCK)
+        near[part, :] = dot(adj_fore[part, :], message[part, :])
     for copy in sent:
         copy.wait_recv()
     for copy in crs_copies:
@@ -228,8 +230,7 @@
 
     loads["w_update"].wait()
     agg_t = dot(reach[...], message[...])
-    agg_t += dot(reach_crs[...], coarse_all[...])
-    agg_t = (agg_t + dot(echo[...], land_one[...])).astype(jnp.bfloat16)
+    agg_t = (agg_t + dot(reach_far[...], landed[...])).astype(jnp.bfloat16)
     pre_t = dot(agg_t, w_update[...])
     g = gate(pre_t)
     d_t = (live_t * cot_t * (g * (1.0 + pre_t * (1.0 - g)))).astype(jnp.bfloat16)
@@ -238,9 +239,7 @@
 
     for b in range(blocks):
         part = pl.ds(b * BLOCK, BLOCK)
-        total = dot(adj_fore[part, :], message[part, :])
-        total += dot(spread[part, :], land_one[...])
-        total += dot(picker[part, :], coarse_all[...])
+        total = near[part, :] + dot(far_fore[part, :], landed[...])
         aggregate[part, :] = total.astype(jnp.bfloat16)
 
     for start in range(0, rows, STEP):
@@ -375,13 +374,13 @@
         vmem((rows, tiles), bf16),
         vmem((tiles, rows), bf16),
         vmem((tiles, rows), bf16),
-        vmem((tiles, tiles), bf16),
-        vmem((tiles, group), bf16),
-        vmem((rows, group), bf16),
+        vmem((tiles, tiles + group), bf16),
+        vmem((rows, tiles + group), bf16),
         vmem((group, rows), bf16),
         vmem((rows, hidden), bf16),
         vmem((rows, hidden), f32),
         vmem((c_rows, hidden), f32),
+        vmem((rows, hidden), f32),
         vmem((rows, hidden), bf16),
         vmem((rows, hidden), bf16),
         vmem((rows, hidden), bf16),
@@ -391,8 +390,7 @@
         vmem((tiles, hidden), bf16),
         vmem((tiles, hidden), bf16),
         vmem((tiles, hidden), bf16),
-        vmem((tiles, hidden), bf16),
-        vmem((group, hidden), bf16),
+        vmem((tiles + group, hidden), bf16),
         vmem((group, hidden), f32),
         vmem((group, hidden), bf16),
         vmem((n_lvl - 1, c_rows, hidden), bf16),

time: 20.5 us -> 19.9 us (0.971)
  Pallas kernels: 19 us -> 18.4 us
    pallas_call x1, Pallas kernels: 16.8 us -> 16.2 us  [on_device(): pl.pallas_call(functools.partial(layer_kernel, n_dom, n_lvl), out_shape=o...]
where the time goes in v4:
time: 19.9 us; the launch traced here: 19.7 us
  Pallas kernels  18.4 us (92%)
  between operations  1.29 us (6%)
    pallas_call x1, Pallas kernels, on_device(): pl.pallas_call(functools.partial(layer_kernel, n_dom, n_lvl), out_shape=o...  16.2 us
    pallas_call x1, Pallas kernels, on_device(): pl.pallas_call(store_kernel, out_shape=outs, in_specs=[far] * 3, out_spec...  2.22 us

profile of v4, /device:TPU:0, one launch (start us, length us, event | category | flops | bytes accessed | tf_op | source)
XLA Modules:
  0.0 19.7 jit_solution(505781024244170204)
XLA Ops:
  1.3 16.2 %layer.1 = (bf16[768,512]{1,0:T(8,128)(2,1)}, bf16[768,512]{1,0:T(8,128)(2,1)}, bf16[64,512]{1,0:T(8,128)(2,1)}) custom-call(bf16[768,512]{1,0:T(8,128)(2,1)} %node_hbm.1, bf16[64,512]{1,0:T(8,128)(2,1)} %coarse_hbm.1, bf16[768,512]{1,0:T(8,128)(2,1)} %cot_hbm.1, bf16[512,512]{1,0:T(8,128)(2,1)} %w_message_hbm.1, bf16[512,512]{1,0:T(8,128)(2,1)} %w_coarse_hbm.1, ...), custom_call_target="tpu_custom_call" | custom-call | tf_op jit(solution)/shard_map/layer/pallas_call | solution.py:413
  17.5 2.2 %store.1 = (bf16[768,512]{1,0:T(8,128)(2,1)}, bf16[768,512]{1,0:T(8,128)(2,1)}, bf16[64,512]{1,0:T(8,128)(2,1)}) custom-call(bf16[768,512]{1,0:T(8,128)(2,1)} %get-tuple-element.6.updated, bf16[768,512]{1,0:T(8,128)(2,1)} %get-tuple-element.7.d_nodes, bf16[64,512]{1,0:T(8,128)(2,1)} %get-tuple-element.8.d_coarse), custom_call_target="tpu_custom_call" | custom-call | tf_op jit(solution)/shard_map/store/pallas_call | solution.py:436

commit v5 on v4

--- a/solution.py
+++ b/solution.py
@@ -275,13 +275,15 @@
         copy.start()
         grad_copies.append(copy)
 
+    for b in range(blocks):
+        part = pl.ds(b * BLOCK, BLOCK)
+        near[part, :] = dot(adj_back[:, part], d_agg[part, :])
     for copy in sent_two:
         copy.wait_recv()
     for start in range(0, rows, STEP):
         for b in range(start // BLOCK, (start + STEP) // BLOCK):
             part = pl.ds(b * BLOCK, BLOCK)
-            total = dot(adj_back[:, part], d_agg[part, :])
-            total += dot(spread[part, :], land_two[...])
+            total = near[part, :] + dot(spread[part, :], land_two[...])
             d_pre[part, :] = (total * slope_msg[part, :]).astype(jnp.bfloat16)
         part = pl.ds(start, STEP)
         d_nodes[part, :] = (

time: 19.9 us -> 19.9 us (level)
  no operation moved by 1% of the time
where the time goes in v5:
time: 19.9 us; the launch traced here: 19.7 us
  Pallas kernels  18.4 us (92%)
  between operations  1.29 us (6%)
    pallas_call x1, Pallas kernels, on_device(): pl.pallas_call(functools.partial(layer_kernel, n_dom, n_lvl), out_shape=o...  16.2 us
    pallas_call x1, Pallas kernels, on_device(): pl.pallas_call(store_kernel, out_shape=outs, in_specs=[far] * 3, out_spec...  2.22 us

profile of v5, /device:TPU:0, one launch (start us, length us, event | category | flops | bytes accessed | tf_op | source)
XLA Modules:
  0.0 19.7 jit_solution(11958834176088738611)
XLA Ops:
  1.3 16.2 %layer.1 = (bf16[768,512]{1,0:T(8,128)(2,1)}, bf16[768,512]{1,0:T(8,128)(2,1)}, bf16[64,512]{1,0:T(8,128)(2,1)}) custom-call(bf16[768,512]{1,0:T(8,128)(2,1)} %node_hbm.1, bf16[64,512]{1,0:T(8,128)(2,1)} %coarse_hbm.1, bf16[768,512]{1,0:T(8,128)(2,1)} %cot_hbm.1, bf16[512,512]{1,0:T(8,128)(2,1)} %w_message_hbm.1, bf16[512,512]{1,0:T(8,128)(2,1)} %w_coarse_hbm.1, ...), custom_call_target="tpu_custom_call" | custom-call | tf_op jit(solution)/shard_map/layer/pallas_call | solution.py:415
  17.5 2.2 %store.1 = (bf16[768,512]{1,0:T(8,128)(2,1)}, bf16[768,512]{1,0:T(8,128)(2,1)}, bf16[64,512]{1,0:T(8,128)(2,1)}) custom-call(bf16[768,512]{1,0:T(8,128)(2,1)} %get-tuple-element.6.updated, bf16[768,512]{1,0:T(8,128)(2,1)} %get-tuple-element.7.d_nodes, bf16[64,512]{1,0:T(8,128)(2,1)} %get-tuple-element.8.d_coarse), custom_call_target="tpu_custom_call" | custom-call | tf_op jit(solution)/shard_map/store/pallas_call | solution.py:438
